TPU v7x, 128 devices: a whole 4x4x4 slice. The times are simulated.
128 devices in a mesh: cache: 32 (over y, x, core), psg: 4 (over z).
Axes of the slice: x: 4, y: 4, z: 4, core: 2. Of those that a mesh axis runs over, the one named last changes fastest.
Arguments:
- question_ids: int32 [32, 16], P('cache'), may hold values from 0 to 32127
- answer_ids: int32 [32, 32], P('cache'), may hold values from 0 to 32127
- owner: int32 [32, 32, 1], P('cache', 'psg'), may hold values from 0 to 31; in each aligned block of 32 rows (0 to 31, 32 to 63, ..., all dimensions but the last counted through in order) at most 2 rows name the same one
- slot: int32 [32, 32], P('cache', 'psg'), may hold values from 0 to 31
- passage_score: float32 [32, 32], P('cache', 'psg'), may hold values from -4 to 304
- memory: bfloat16 [1024, 16, 4096], P('cache', None, 'psg'), may hold values from -64 to 64
- embedding: bfloat16 [32128, 4096], P('cache', 'psg'), may hold values from -6 to 6
- live_gain: float32 [4096], replicated, may hold values from 0.1 to 1.9
- live_qkv: bfloat16 [4096, 3, 2048], P(None, None, 'psg'), may hold values from -0.09375 to 0.09375
- rel_bias: float32 [32, 32], P('psg'), may hold values from -6 to 306
- live_out: bfloat16 [2048, 4096], P('psg'), may hold values from -0.375 to 0.375
- enc_gain: float32 [4096], replicated, may hold values from 0.1 to 1.9
- cross_kv: bfloat16 [4096, 2, 2048], P(None, None, 'psg'), may hold values from -0.09375 to 0.09375
- dec_gain: float32 [4096], replicated, may hold values from 0.1 to 1.9
- cross_query: bfloat16 [4096, 2048], P(None, 'psg'), may hold values from -0.09375 to 0.09375
- cross_out: bfloat16 [2048, 4096], P('psg'), may hold values from -0.375 to 0.375
Outputs:
- encoded: bfloat16 [32, 32, 32, 4096], P('cache', 'psg')
- decoded: bfloat16 [32, 32, 4096], P('cache', None, 'psg')
Inputs may be any that keep to these rules, and one draw needn't show every extreme that they name: Among the 32 passages of one question at most 2 have the same owner, and in some question an owner has exactly 2.
All inputs are finite; a program needn't handle non-finite values.
Results may differ from a plain program's by a relative error of at most 0.025.
Values may be sent and summed in bfloat16 or wider, within the bound.
A program may use at most 192 MiB of HBM per device.

v0:
```python
import functools

import jax
import jax.numpy as jnp
import numpy as np
from jax import lax
from jax.experimental import pallas as pl
from jax.experimental.pallas import tpu as pltpu
from jax.sharding import PartitionSpec as P

HEAD = 64
EPSILON = 1e-06
F32 = jnp.float32
BF16 = jnp.bfloat16


def bucket_table(length, bucket_count):
    positions = np.arange(length)
    relative = positions[None, :] - positions[:, None]
    halfway = bucket_count // 2
    exact_span = halfway // 2
    upper_side = (relative > 0).astype(np.int64) * halfway
    distance = np.abs(relative)
    log_bucket = exact_span + (
        np.log(np.maximum(distance, 1) / exact_span)
        / np.log(128.0 / exact_span)
        * (halfway - exact_span)
    ).astype(np.int64)
    log_bucket = np.minimum(log_bucket, halfway - 1)
    return upper_side + np.where(distance < exact_span, distance, log_bucket)


def spread_table(length, bucket_count):
    buckets = np.tile(bucket_table(length, bucket_count).T, (1, 4)).reshape(-1)
    return (buckets[None, :] == np.arange(bucket_count)[:, None]).astype(np.float32)


def dot32(a, b, dims):
    return lax.dot_general(a, b, (dims, ((), ())), preferred_element_type=F32)


MESH = pl.DeviceIdType.MESH
VM = pl.BlockSpec(memory_space=pltpu.VMEM)
SM = pl.BlockSpec(memory_space=pltpu.SMEM)
ANY = pl.BlockSpec(memory_space=pl.ANY)


def params(collective_id, mib):
    return pltpu.CompilerParams(
        collective_id=collective_id, has_side_effects=True, vmem_limit_bytes=mib << 20
    )


class Place:
    def __init__(self):
        self.c = lax.axis_index("cache")
        self.z = lax.axis_index("psg")
        self.core = lax.rem(self.c, 2)
        self.x = lax.rem(lax.div(self.c, 2), 4)
        self.y = lax.div(self.c, 8)

    def cache(self, c):
        return {"cache": c, "psg": self.z}

    def chip(self, y, x):
        return self.cache((y * 4 + x) * 2 + self.core)

    def sibling(self):
        return self.cache(self.c + 1 - 2 * self.core)

    def up(self, z):
        return {"cache": self.c, "psg": z}


def turn(p, k):
    return lax.rem(p + k + 4, 4)


def greet_all(at):
    barrier = pltpu.get_barrier_semaphore()

    def greet(d, carry):
        pl.semaphore_signal(
            barrier, inc=1, device_id=at.cache(lax.rem(at.c + d, 32)), device_id_type=MESH
        )
        return carry

    lax.fori_loop(1, 32, greet, 0)
    for k in range(1, 4):
        pl.semaphore_signal(barrier, inc=1, device_id=at.up(turn(at.z, k)), device_id_type=MESH)
    pl.semaphore_wait(barrier, 34)


class Mover:
    def __init__(self, send, recv):
        self.send, self.recv, self.count, self.started = send, recv, 0, []

    def go(self, src, dst, device):
        i = self.count
        self.count += 1
        copy = pltpu.make_async_remote_copy(
            src_ref=src, dst_ref=dst, send_sem=self.send.at[i], recv_sem=self.recv.at[i],
            device_id=device, device_id_type=MESH,
        )
        copy.start()
        self.started.append(copy)
        return copy

    def finish_sends(self):
        for copy in self.started:
            copy.wait_send()


class Ring:
    def __init__(self, mover, pos, device, own, dst, units, start=True):
        self.mover, self.pos, self.device, self.own, self.dst = mover, pos, device, own, dst
        self.right, self.left = device(turn(pos, 1)), device(turn(pos, -1))
        self.to_right, self.to_left, self.far = {}, {}, {}
        half = len(units) // 2
        self.first, self.last = units[:half], units[half:]
        if start:
            for u, v in zip(units, self.last + self.first):
                self.begin_right(u)
                self.begin_left(v)

    def begin_right(self, u):
        self.to_right[u] = self.mover.go(self.own(u), self.dst(self.pos, u, 1), self.right)

    def begin_left(self, u):
        self.to_left[u] = self.mover.go(self.own(u), self.dst(self.pos, u, -1), self.left)

    def pass_right(self, u):
        self.to_right[u].wait_recv()
        before = turn(self.pos, -1)
        self.far[u] = self.mover.go(self.dst(before, u, 1), self.dst(before, u, 2), self.right)

    def pass_left(self, u):
        self.to_left[u].wait_recv()
        after = turn(self.pos, 1)
        self.far[u] = self.mover.go(self.dst(after, u, -1), self.dst(after, u, 2), self.left)

    def onward(self):
        for u, v in zip(self.first, self.last):
            self.pass_right(u)
            self.pass_left(v)

    def near(self):
        for u in self.last:
            self.to_right[u].wait_recv()
        for v in self.first:
            self.to_left[v].wait_recv()

    def end(self):
        for copy in self.far.values():
            copy.wait_recv()


class Spread:
    def __init__(self, at, mover, full, width):
        self.at, self.mover, self.full = at, mover, full
        self.quarter, self.width = width // 4, width

    def begin(self, live_out, first):
        at = self.at
        rows = pl.ds(pl.multiple_of(at.c * 16, 16), 16)
        self.start = [
            self.mover.go(
                live_out.at[rows, pl.ds(first, self.width)],
                self.full.at[k - 1, at.y, at.x, at.core],
                at.up(turn(at.z, -k)),
            )
            for k in range(1, 4)
        ]

    def cols(self, u, n=1):
        return pl.ds(u * self.quarter, n * self.quarter)

    def phase_one(self):
        at, full = self.at, self.full
        for copy in self.start:
            copy.wait_recv()
        a = lambda pos, u, k=0: full.at[:, at.y, pos, at.core, :, self.cols(u)]
        b = lambda pos, u, k=0: full.at[:, pos, at.x, at.core, :, self.cols(u)]
        self.one = [
            Ring(self.mover, at.x, lambda p: at.chip(at.y, p), lambda u: a(at.x, u), a, [0, 1]),
            Ring(self.mover, at.y, lambda p: at.chip(p, at.x), lambda u: b(at.y, u), b, [2, 3]),
        ]

    def phase_one_onward(self):
        for ring in self.one:
            ring.onward()

    def phase_one_end(self):
        for ring in self.one:
            ring.near()
            ring.end()

    def line(self, full, axis):
        at = self.at
        if axis == "x":
            return full.at[:, at.y, :, at.core, :, self.cols(0, 2)]
        return full.at[:, :, at.x, at.core, :, self.cols(2, 2)]

    def phase_two(self):
        at, full = self.at, self.full
        a = lambda pos, u, k=0: full.at[:, pos, :, at.core, :, self.cols(u)]
        b = lambda pos, u, k=0: full.at[:, :, pos, at.core, :, self.cols(u)]
        self.two = [
            Ring(self.mover, at.y, lambda p: at.chip(p, at.x), lambda u: a(at.y, u), a, [0, 1]),
            Ring(self.mover, at.x, lambda p: at.chip(at.y, p), lambda u: b(at.x, u), b, [2, 3]),
        ]
        self.over = []
        self.cross(0)

    def cross(self, k):
        at, full = self.at, self.full
        a = full.at[:, turn(at.y, k), :, at.core, :, self.cols(0, 2)]
        b = full.at[:, :, turn(at.x, k), at.core, :, self.cols(2, 2)]
        for view in (a, b):
            self.over.append(self.mover.go(view, view, at.sibling()))

    def phase_two_onward(self):
        for ring in self.two:
            ring.onward()
        for ring in self.two:
            ring.near()
        self.cross(1)
        self.cross(-1)

    def finish(self):
        for ring in self.two:
            ring.end()
        self.cross(2)
        for copy in self.over:
            copy.wait_recv()


def norm_rows(rows, gain):
    wide = rows.astype(F32)
    inverse = lax.rsqrt(jnp.mean(wide * wide, axis=-1, keepdims=True) + EPSILON)
    return (wide * gain).astype(BF16), inverse


def fetch_kernel(
    question_ids, answer_ids, owner, slot, rel_bias, spread_of, memory, embedding, own_score,
    live_out, w_qkv, cross_kv, cross_query,
    live_gain, enc_gain, dec_gain,
    x_out, tokens, scores, full, full_next, proj_mem, proj_q, qg, w_val_out, bias,
    line_buf, score, by_key, every, table, turned, plan, tok, table_w, out_buf, in_buf0, in_buf1, in_buf2, in_buf3, own, pair_buf, a_buf, b_buf, a2_buf, b2_buf, tok_sum,
    x_full, weights, acc, squares, scaled, w_query, kv_buf, w_key, w_val,
    send, recv, a2a_send, a2a_recv, line_send, line_recv, local_sem, kv_sem, out_sem,
):
    at = Place()
    line_buf[...] = jnp.zeros((8, 128), jnp.int32)
    line_buf[0:1, 0:8] = owner[...]
    line_buf[0:1, 32:40] = slot[...]
    line_buf[1:2, 64:80] = question_ids[...]
    line_buf[1:2, 80:112] = answer_ids[...]
    placed = pltpu.roll(line_buf[0:1], 8 * at.z, 1)
    every[at.c, at.z] = placed + jnp.where(at.z == 0, line_buf[1:2], 0)
    score[...] = jnp.zeros((1, 128), F32)
    score[:, 0:8] = own_score[...]
    table[32:128] = jnp.zeros((96, 128), jnp.int32)
    load_table = pltpu.make_async_copy(embedding, table_w, local_sem.at[5])
    load_table.start()
    load_weights = [
        pltpu.make_async_copy(w_qkv.at[i], weights.at[i], local_sem.at[i]) for i in range(3)
    ] + [pltpu.make_async_copy(cross_query, w_query, local_sem.at[3])]
    for copy in load_weights:
        copy.start()

    def kv_copy(i):
        slot = lax.rem(i, 4)
        return pltpu.make_async_copy(
            cross_kv.at[pl.ds(i * 256, 256)], kv_buf.at[slot], kv_sem.at[slot]
        )

    for i in range(3):
        kv_copy(i).start()

    def split_kv(first, last):
        def one(i, carry):
            @pl.when(i < 13)
            def _():
                kv_copy(i + 3).start()

            kv_copy(i).wait()
            rows = pl.ds(pl.multiple_of(i * 256, 256), 256)
            slot = lax.rem(i, 4)
            w_key[rows] = kv_buf[slot, :, 0, :]
            gain = jnp.transpose(jnp.broadcast_to(enc_gain[:, rows], (128, 256)))[:, 0:1]
            w_val[rows] = (kv_buf[slot, :, 1, :].astype(F32) * gain).astype(BF16)
            return carry

        lax.fori_loop(first, last, one, 0)

    greet_all(at)
    mover = Mover(send, recv)
    in_buf = (in_buf0, in_buf1, in_buf2, in_buf3)

    near = [
        mover.go(every.at[at.c, at.z], every.at[at.c, at.z], at.up(turn(at.z, k)))
        for k in range(1, 4)
    ]

    def line_copy(d):
        return pltpu.make_async_remote_copy(
            src_ref=every.at[at.c], dst_ref=every.at[at.c], send_sem=line_send.at[d],
            recv_sem=line_recv.at[d], device_id=at.cache(lax.rem(at.c + d, 32)),
            device_id_type=MESH,
        )

    def send_line(d, carry):
        line_copy(d).start()
        return carry

    def wait_line(d, carry):
        line_copy(d).wait()
        return carry

    for copy in near:
        copy.wait_recv()
    lax.fori_loop(1, 32, send_line, 0)
    spread = Spread(at, mover, full, 2048)
    spread.begin(live_out, 0)
    spread_next = Spread(at, mover, full_next, 2048)
    spread_next.begin(live_out, 2048)
    lax.fori_loop(1, 32, wait_line, 0)
    for q in range(32):
        table[q : q + 1] = (every[q, 0] + every[q, 1]) + (every[q, 2] + every[q, 3])

    names = table[0:32]
    turned[...] = jnp.transpose(table[...].astype(F32))
    lane = lax.broadcasted_iota(jnp.int32, (32, 128), 1)
    rank = jnp.zeros((32, 128), jnp.int32)
    for shift in range(1, 32):
        same = jnp.logical_and(pltpu.roll(names, shift, 1) == names, lane >= shift)
        rank = rank + jnp.where(same, 1, 0)
    entries = pltpu.roll(names, 96, 1)
    found = []
    for r in range(2):
        hit = jnp.logical_and(jnp.logical_and(names == at.c, rank == r), lane < 32)
        entry = jnp.where(hit, entries, 0)
        for shift in (64, 32, 16, 8, 4, 2, 1):
            entry = entry + pltpu.roll(entry, shift, 1)
        found.append(entry)
    asks = jnp.where(lane == 32, found[0], found[1])
    table[0:32] = jnp.where(lane < 32, names * 2 + rank, asks)
    to_plan = pltpu.make_async_copy(table.at[pl.ds(0, 32)], plan, local_sem.at[6])
    to_plan.start()
    to_plan.wait()

    def passage_copy(h, d):
        q = lax.rem(at.c + d, 32)
        return pltpu.make_async_remote_copy(
            src_ref=out_buf.at[h, pl.ds(2 * q, 2)], dst_ref=in_buf[h].at[pl.ds(2 * at.c, 2)],
            send_sem=a2a_send.at[h, d], recv_sem=a2a_recv.at[h, d],
            device_id=at.cache(q), device_id_type=MESH,
        )

    def send_part(h):
        lanes = pl.ds(h * 256, 256)

        def one(d, carry):
            q = lax.rem(at.c + d, 32)
            out_buf[h, 2 * q] = memory[plan[q, 32], :, lanes]
            out_buf[h, 2 * q + 1] = memory[plan[q, 33], :, lanes]
            passage_copy(h, d).start()
            return carry

        lax.fori_loop(1, 32, one, 0)
        in_buf[h][2 * at.c] = memory[plan[at.c, 32], :, lanes]
        in_buf[h][2 * at.c + 1] = memory[plan[at.c, 33], :, lanes]

    def wait_part(h):
        def one(d, carry):
            passage_copy(h, d).wait_recv()
            return carry

        lax.fori_loop(1, 32, one, 0)

        def pack(j, carry):
            own[h, pl.ds(pl.multiple_of(16 * j, 16), 16)] = in_buf[h][plan[at.c, j]]
            return carry

        lax.fori_loop(0, 32, pack, 0)

    def lanes_of(pos, h):
        return pl.ds(pl.multiple_of(pos * 1024 + h * 512, 512), 512)

    def part(pos, unit, k=0):
        h, g = unit
        return x_full.at[
            pl.ds(g * 256, 256), pl.ds(pl.multiple_of(pos * 1024 + h * 256, 256), 256)
        ]

    def ring_part(h):
        return Ring(
            mover, at.z, at.up, lambda u: own.at[u[0], pl.ds(u[1] * 256, 256)], part,
            [(h, 0), (h, 1)],
        )

    stored = []

    def multiply(k, h):
        pos = turn(at.z, k)
        lanes = lanes_of(pos, h)
        if k == 0:
            x_full[:, lanes] = jnp.concatenate([own[2 * h], own[2 * h + 1]], axis=1)
        keep = pltpu.make_async_copy(
            x_full.at[:, lanes], x_out.at[:, lanes], out_sem.at[len(stored)]
        )
        keep.start()
        first = not stored
        stored.append(keep)
        gain = live_gain[:, lanes]
        for r in range(2):
            rows = pl.ds(r * 256, 256)
            wide = x_full[rows, lanes].astype(F32)
            scaled[rows] = (wide * gain).astype(BF16)
            square = jnp.sum(wide * wide, axis=1, keepdims=True)
            squares[rows] = square if first else squares[rows] + square

        def one(i, carry):
            product = jnp.dot(scaled[...], weights[i, lanes], preferred_element_type=F32)
            acc[i] = product if first else acc[i] + product
            return carry

        lax.fori_loop(0, 3, one, 0)

    def sent_part(h):
        def one(d, carry):
            passage_copy(h, d).wait_send()
            return carry

        lax.fori_loop(1, 32, one, 0)

    send_part(0)

    load_table.wait()
    held = lax.broadcasted_iota(jnp.int32, (48, 1004), 1).astype(F32) + (at.c * 1004).astype(F32)
    for b in range(8):
        picks = [
            jnp.where(held == turned[64:112, q : q + 1], 1.0, 0.0).astype(BF16)
            for q in range(4 * b, 4 * b + 4)
        ]
        named = jnp.dot(
            jnp.concatenate(picks, axis=0), table_w[...], preferred_element_type=F32
        ).astype(BF16)
        for n in range(4):
            q = 4 * b + n
            tok[q // 8, (q // 2) % 4, q % 2] = named[48 * n : 48 * (n + 1)]
    other = 1 - at.core
    pair = mover.go(tok.at[:, :, other], pair_buf, at.sibling())
    split_kv(0, 3)
    sent_part(0)
    send_part(1)

    pair.wait_recv()

    def add_pair(y, carry):
        for x in range(4):
            pair_buf[y, x] = pair_buf[y, x] + tok[y, x, at.core]
        return carry

    lax.fori_loop(0, 4, add_pair, 0)
    wait_part(0)
    rings = [ring_part(0)]
    sent_part(1)
    send_part(2)
    lo, hi = pl.ds(0, 512), pl.ds(512, 512)
    tok_a = [
        mover.go(
            pair_buf.at[:, turn(at.x, k), :, lo], a_buf.at[k - 1], at.chip(at.y, turn(at.x, k))
        )
        for k in range(1, 4)
    ]
    tok_b = [
        mover.go(
            pair_buf.at[turn(at.y, k), :, :, hi], b_buf.at[k - 1], at.chip(turn(at.y, k), at.x)
        )
        for k in range(1, 4)
    ]
    near_scores = [
        mover.go(score, scores.at[at.z], at.up(turn(at.z, k))) for k in range(1, 4)
    ]
    scores[at.z] = score[...]
    wait_part(1)
    rings.append(ring_part(1))
    for copy in load_weights:
        copy.wait()
    multiply(0, 0)
    sent_part(2)
    send_part(3)
    split_kv(3, 6)
    for copy in tok_a + tok_b:
        copy.wait_recv()

    def add_line(i, carry):
        a_buf[0, i] = (a_buf[0, i] + a_buf[1, i]) + (a_buf[2, i] + pair_buf[i, at.x, :, lo])
        b_buf[0, i] = (b_buf[0, i] + b_buf[1, i]) + (b_buf[2, i] + pair_buf[at.y, i, :, hi])
        return carry

    lax.fori_loop(0, 4, add_line, 0)
    tok_a2 = [
        mover.go(a_buf.at[0, turn(at.y, k)], a2_buf.at[k - 1], at.chip(turn(at.y, k), at.x))
        for k in range(1, 4)
    ]
    tok_b2 = [
        mover.go(b_buf.at[0, turn(at.x, k)], b2_buf.at[k - 1], at.chip(at.y, turn(at.x, k)))
        for k in range(1, 4)
    ]
    wait_part(2)
    rings.append(ring_part(2))
    rings[0].onward()
    wait_part(3)
    rings.append(ring_part(3))
    for copy in tok_a2 + tok_b2:
        copy.wait_recv()
    tok_sum[:, lo] = (a2_buf[0] + a2_buf[1]) + (a2_buf[2] + a_buf[0, at.y])
    tok_sum[:, hi] = (b2_buf[0] + b2_buf[1]) + (b2_buf[2] + b_buf[0, at.x])
    mine = pl.ds(pl.multiple_of(at.z * 1024, 1024), 1024)
    near_tokens = [
        mover.go(tok_sum, tokens.at[:, mine], at.up(turn(at.z, k))) for k in range(1, 4)
    ]
    tokens[:, mine] = tok_sum[...]
    rings[1].onward()
    spread.phase_one()
    spread_next.phase_one()
    multiply(0, 1)
    split_kv(6, 8)
    rings[0].near()
    rings[1].near()
    multiply(1, 0)
    spread.phase_one_onward()
    multiply(-1, 0)
    split_kv(8, 10)
    rings[2].onward()
    spread.phase_one_end()
    spread.phase_two()
    spread_next.phase_one_onward()
    split_kv(10, 13)
    rings[3].onward()
    rings[0].end()
    rings[1].end()
    multiply(2, 0)
    spread.phase_two_onward()
    split_kv(13, 16)
    def spread_bias(b, carry):
        cols = pl.ds(pl.multiple_of(b * 128, 128), 128)
        by_key[b] = jnp.dot(
            rel_bias[...], spread_of[:, cols], precision=lax.Precision.HIGHEST,
            preferred_element_type=F32,
        )
        return carry

    lax.fori_loop(0, 32, spread_bias, 0)
    for h in range(8):
        bias[h] = by_key[:, h, :]
    keep_values = pltpu.make_async_copy(w_val, w_val_out, local_sem.at[4])
    keep_values.start()
    for copy in near_scores + near_tokens:
        copy.wait_recv()

    rows, inverse = norm_rows(tokens[0:16], live_gain[...])

    def project(i, carry):
        total = jnp.dot(rows, weights[i], preferred_element_type=F32)
        proj_q[i] = (total * inverse).astype(BF16)
        return carry

    lax.fori_loop(0, 3, project, 0)
    rows_a, inverse_a = norm_rows(tokens[16:48], dec_gain[...])
    queries = jnp.dot(rows_a, w_query[...], preferred_element_type=F32) * inverse_a
    head = lax.broadcasted_iota(jnp.int32, (32, 512), 1) // HEAD
    for h in range(8):
        scaled[pl.ds(32 * h, 32)] = jnp.where(head == h, queries, 0.0).astype(BF16)

    def fold(n, carry):
        cols = pl.ds(pl.multiple_of(n * 1024, 1024), 1024)
        product = dot32(scaled[pl.ds(0, 256)], w_key[cols], ((1,), (1,)))
        qg[:, cols] = (product * enc_gain[:, cols]).astype(BF16)
        return carry

    lax.fori_loop(0, 4, fold, 0)
    rings[2].near()
    rings[3].near()
    multiply(1, 1)
    multiply(-1, 1)
    rings[2].end()
    rings[3].end()
    multiply(2, 1)
    inverse_m = lax.rsqrt(squares[...] * (1.0 / 4096) + EPSILON)

    def close(i, carry):
        proj_mem[i] = (acc[i] * inverse_m).astype(BF16)
        return carry

    lax.fori_loop(0, 3, close, 0)
    spread.finish()
    spread_next.phase_one_end()
    for copy in stored:
        copy.wait()
    keep_values.wait()
    mover.finish_sends()

    sent_part(3)


def fetch(*args):
    return pl.pallas_call(
        fetch_kernel,
        out_shape=(
            jax.ShapeDtypeStruct((512, 4096), BF16),
            jax.ShapeDtypeStruct((48, 4096), BF16),
            jax.ShapeDtypeStruct((4, 1, 128), F32),
            jax.ShapeDtypeStruct((3, 4, 4, 2, 16, 2048), BF16),
            jax.ShapeDtypeStruct((3, 4, 4, 2, 16, 2048), BF16),
            jax.ShapeDtypeStruct((3, 512, 512), BF16),
            jax.ShapeDtypeStruct((3, 16, 512), BF16),
            jax.ShapeDtypeStruct((256, 4096), BF16),
            jax.ShapeDtypeStruct((4096, 512), BF16),
            jax.ShapeDtypeStruct((8, 32, 128), F32),
        ),
        in_specs=[VM] * 7 + [ANY, VM, ANY, ANY, ANY, ANY, VM, VM, VM],
        out_specs=(ANY, VM, VM, ANY, ANY, VM, VM, VM, ANY, VM),
        scratch_shapes=[
            pltpu.VMEM((8, 128), jnp.int32), pltpu.VMEM((1, 128), F32),
            pltpu.VMEM((32, 8, 128), F32),
            pltpu.VMEM((32, 4, 1, 128), jnp.int32), pltpu.VMEM((128, 128), jnp.int32),
            pltpu.VMEM((128, 128), F32), pltpu.SMEM((32, 128), jnp.int32),
            pltpu.VMEM((4, 4, 2, 48, 1024), BF16), pltpu.VMEM((1004, 1024), BF16),
            pltpu.VMEM((4, 64, 16, 256), BF16), pltpu.VMEM((64, 16, 256), BF16),
            pltpu.VMEM((64, 16, 256), BF16), pltpu.VMEM((64, 16, 256), BF16),
            pltpu.VMEM((64, 16, 256), BF16),
            pltpu.VMEM((4, 512, 256), BF16), pltpu.VMEM((4, 4, 48, 1024), BF16),
            pltpu.VMEM((3, 4, 48, 512), BF16), pltpu.VMEM((3, 4, 48, 512), BF16),
            pltpu.VMEM((3, 48, 512), BF16), pltpu.VMEM((3, 48, 512), BF16),
            pltpu.VMEM((48, 1024), BF16),
            pltpu.VMEM((512, 4096), BF16), pltpu.VMEM((3, 4096, 512), BF16),
            pltpu.VMEM((3, 512, 512), F32), pltpu.VMEM((512, 1), F32),
            pltpu.VMEM((512, 512), BF16), pltpu.VMEM((4096, 512), BF16),
            pltpu.VMEM((4, 256, 2, 512), BF16), pltpu.VMEM((4096, 512), BF16),
            pltpu.VMEM((4096, 512), BF16),
            pltpu.SemaphoreType.DMA((112,)), pltpu.SemaphoreType.DMA((112,)),
            pltpu.SemaphoreType.DMA((4, 32)), pltpu.SemaphoreType.DMA((4, 32)),
            pltpu.SemaphoreType.DMA((32,)), pltpu.SemaphoreType.DMA((32,)),
            pltpu.SemaphoreType.DMA((7,)), pltpu.SemaphoreType.DMA((4,)),
            pltpu.SemaphoreType.DMA((8,)),
        ],
        compiler_params=params(2, 60),
    )(*args)


def reader_kernel(
    proj_mem, proj_q, bias, x_mem, tokens, qg, scores, left_in, right_in, live_out, w_val_in,
    cross_out_in,
    encoded, decoded,
    ctx, others, x_seq, left, right, own_out, w_val, w_out, ql, ql_part, lv, lv_part, s, w, values,
    inv, parts, part_buf, send, recv, local_sem,
):
    at = Place()
    mover = Mover(send, recv)
    spread = Spread(at, mover, right, 2048)
    loads = [
        pltpu.make_async_copy(a, b, local_sem.at[i])
        for i, (a, b) in enumerate([
            (spread.line(right_in, "x"), spread.line(right, "x")),
            (spread.line(right_in, "y"), spread.line(right, "y")),
            (x_mem, x_seq.at[:, pl.ds(0, 16)]), (live_out, own_out), (w_val_in, w_val),
            (left_in, left), (cross_out_in, w_out),
        ])
    ]
    for copy in loads:
        copy.start()
    greet_all(at)
    scale = HEAD ** (-0.5)
    nt = ((1,), (1,))
    loads[0].wait()
    loads[1].wait()
    spread.phase_two()

    def chunk(j):
        return pl.ds(pl.multiple_of(j * 256, 256), 256)

    def part(pos, u, k):
        return others.at[{1: 2, -1: 0, 2: 1}[k], chunk(turn(pos, u))]

    ring = Ring(
        mover, at.z, at.up, lambda u: ctx.at[chunk(turn(at.z, u))], part, [2, 1, 3, 0], False
    )

    low = lax.broadcasted_iota(jnp.int32, (128, 128), 1) < HEAD
    eye = lax.broadcasted_iota(jnp.int32, (128, 128), 0)
    eye = eye == lax.broadcasted_iota(jnp.int32, (128, 128), 1)
    eye = jnp.where(eye, 1.0, 0.0).astype(BF16)
    owner_lane = lax.broadcasted_iota(jnp.int32, (32, 128), 1) // 32

    def attend(j):
        def group(g, carry):
            first = j * 8 + g * 4

            def pair(i, p):
                lanes = pl.ds(128 * p, 128)
                pieces = []
                for n in range(4):
                    pieces.append(
                        proj_mem[i, pl.ds(pl.multiple_of((first + n) * 16, 16), 16), lanes]
                    )
                    pieces.append(proj_q[i, :, lanes])
                return jnp.concatenate(pieces, axis=0)

            for p in range(4):
                q, k, v = pair(0, p), pair(1, p), pair(2, p)
                both = []
                for e in range(2):
                    keep = low if e == 0 else jnp.logical_not(low)
                    full = dot32(k, jnp.where(keep, q, jnp.zeros_like(q)), nt)
                    sc = full[0:32]
                    for n in range(1, 4):
                        sc = jnp.where(owner_lane == n, full[32 * n : 32 * n + 32], sc)
                    sc = sc * scale + bias[2 * p + e]
                    ex = jnp.exp(sc - jnp.max(sc, axis=0, keepdims=True))
                    ex = ex * (1.0 / jnp.sum(ex, axis=0, keepdims=True))
                    full = jnp.concatenate(
                        [jnp.where(owner_lane == n, ex, 0.0) for n in range(4)], axis=0
                    ).astype(BF16)
                    by_query = dot32(eye, full, nt).astype(BF16)
                    both.append(jnp.dot(by_query, v, preferred_element_type=F32))
                ctx[pl.ds(pl.multiple_of(first * 32, 128), 128), pl.ds(128 * p, 128)] = jnp.where(
                    low, both[0], both[1]
                ).astype(BF16)
            return carry

        lax.fori_loop(0, 2, group, 0)

    for u in (2, 3, 1, 0):
        attend(turn(at.z, u))
        ring.begin_right(u)
        ring.begin_left(u)

    loads[2].wait()

    def fill(p, carry):
        x_seq[p, pl.ds(16, 16)] = tokens[pl.ds(0, 16)]
        return carry

    lax.fori_loop(0, 32, fill, 0)
    ring.pass_right(2)

    def rows_of(j):
        return x_seq[pl.ds(j * 8, 8)].reshape(256, 4096)

    def score_inputs(j, carry):
        s[j] = dot32(qg[...], rows_of(j), nt)
        return carry

    lax.fori_loop(0, 4, score_inputs, 0)
    ring.pass_left(3)
    spread.phase_two_onward()
    loads[4].wait()
    of_question = jnp.dot(tokens[pl.ds(0, 16)], w_val[...], preferred_element_type=F32)

    def value_inputs(j, carry):
        rows = jnp.dot(
            x_seq[pl.ds(j * 8, 8), pl.ds(0, 16)].reshape(128, 4096), w_val[...],
            preferred_element_type=F32,
        )
        for p in range(8):
            values[j, pl.ds(32 * p, 16)] = rows[16 * p : 16 * p + 16]
            values[j, pl.ds(32 * p + 16, 16)] = of_question
        return carry

    lax.fori_loop(0, 4, value_inputs, 0)
    ring.pass_right(1)
    loads[3].wait()
    ql[0] = dot32(qg[...], own_out[...], nt).astype(BF16)
    lv[0] = jnp.dot(own_out[...], w_val[...], preferred_element_type=F32).astype(BF16)

    def absorb(j, k, rows):
        s[j] = s[j] + dot32(ql[k], rows, nt)
        values[j] = values[j] + jnp.dot(rows, lv[k], preferred_element_type=F32)

    def absorb_own(j, carry):
        absorb(j, 0, ctx[chunk(j)])
        return carry

    lax.fori_loop(0, 4, absorb_own, 0)
    loads[5].wait()
    half, rest = pl.ds(0, 2048), pl.ds(2048, 2048)

    def fold_left(k, carry):
        ql_part[k] = dot32(qg[:, half], left[k], nt)
        lv_part[k] = jnp.dot(left[k], w_val[half], preferred_element_type=F32)
        return carry

    lax.fori_loop(0, 3, fold_left, 0)
    ring.pass_left(0)
    spread.finish()

    def fold_right(k, carry):
        rows = right[k].reshape(512, 2048)
        ql[k + 1] = (ql_part[k] + dot32(qg[:, rest], rows, nt)).astype(BF16)
        lv[k + 1] = (
            lv_part[k] + jnp.dot(rows, w_val[rest], preferred_element_type=F32)
        ).astype(BF16)
        return carry

    lax.fori_loop(0, 3, fold_right, 0)

    ring.far[2].wait_recv()
    mine = chunk(at.z)

    def group_rows(k, n):
        if k == 0:
            return own_out[:, pl.ds(n * 1024, 1024)]
        if n < 2:
            return left[k - 1, :, pl.ds(n * 1024, 1024)]
        return right[k - 1, :, :, :, :, pl.ds((n - 2) * 1024, 1024)].reshape(512, 1024)

    squares = jnp.zeros((256, 1), F32)
    for n in range(4):
        cols = pl.ds(n * 1024, 1024)
        attended = None
        for k in range(4):
            rows = ctx[mine] if k == 0 else others[k - 1, mine]
            product = jnp.dot(rows, group_rows(k, n), preferred_element_type=F32)
            product = product.astype(BF16).astype(F32)
            attended = product if k == 0 else attended + product
        own_rows = x_seq[pl.ds(at.z * 8, 8), :, cols].reshape(256, 1024).astype(F32)
        own_rows = (own_rows + attended).astype(BF16)
        encoded[:, cols] = own_rows
        own_rows = own_rows.astype(F32)
        squares = squares + jnp.sum(own_rows * own_rows, axis=1, keepdims=True)
    norm = lax.rsqrt(squares * (1.0 / 4096) + EPSILON)
    inv[at.z] = jnp.transpose(jnp.broadcast_to(norm, (256, 128)))[0:1]
    near = [mover.go(inv.at[at.z], inv.at[at.z], at.up(turn(at.z, k))) for k in range(1, 4)]

    def absorb_other(k, u):
        j = turn(at.z, k + u)
        absorb(j, k, others[k - 1, chunk(j)])

    absorb_other(3, 2)
    absorb_other(1, 3)
    absorb_other(3, 1)
    absorb_other(2, 2)
    ring.to_left[2].wait_recv()
    absorb_other(1, 2)
    ring.to_right[3].wait_recv()
    absorb_other(3, 3)
    ring.to_left[1].wait_recv()
    absorb_other(1, 1)
    absorb_other(1, 0)
    ring.far[3].wait_recv()
    absorb_other(2, 3)
    ring.to_right[0].wait_recv()
    absorb_other(3, 0)
    ring.far[1].wait_recv()
    absorb_other(2, 1)
    ring.far[0].wait_recv()
    absorb_other(2, 0)
    for copy in near:
        copy.wait_recv()

    passage = lax.broadcasted_iota(jnp.int32, (1, 256), 1) // 32
    top = None
    for j in range(4):
        row = jnp.zeros((1, 256), F32)
        line = scores[j]
        for p in range(8):
            row = row + jnp.where(passage == p, line[:, p : p + 1], 0.0)
        total = s[j] * (inv[j] * scale) + row
        s[j] = total
        here = jnp.max(total, axis=1, keepdims=True)
        top = here if top is None else jnp.maximum(top, here)
    sums = jnp.zeros((256, 1), F32)
    for j in range(4):
        ex = jnp.exp(s[j] - top)
        s[j] = ex
        sums = sums + jnp.sum(ex, axis=1, keepdims=True)
    for j in range(4):
        w[j] = (s[j] * inv[j] / sums).astype(BF16)
    heads_out = jnp.zeros((256, 512), F32)
    for j in range(4):
        heads_out = heads_out + jnp.dot(
            w[j], values[j].astype(BF16), preferred_element_type=F32
        )
    head = lax.broadcasted_iota(jnp.int32, (32, 512), 1) // HEAD
    context = jnp.zeros((32, 512), F32)
    for h in range(8):
        context = context + jnp.where(head == h, heads_out[32 * h : 32 * h + 32], 0.0)
    context = context.astype(BF16)
    loads[6].wait()
    for j in range(4):
        parts[j] = jnp.dot(
            context, w_out[:, pl.ds(1024 * j, 1024)], preferred_element_type=F32
        ).astype(BF16)
    last = [
        mover.go(parts.at[turn(at.z, k)], part_buf.at[k - 1], at.up(turn(at.z, k)))
        for k in range(1, 4)
    ]
    for copy in last:
        copy.wait_recv()
    total = parts[at.z].astype(F32)
    for k in range(3):
        total = total + part_buf[k].astype(F32)
    decoded[...] = total.astype(BF16)
    mover.finish_sends()


def reader(*args):
    return pl.pallas_call(
        reader_kernel,
        out_shape=(
            jax.ShapeDtypeStruct((256, 4096), BF16),
            jax.ShapeDtypeStruct((32, 1024), BF16),
        ),
        in_specs=[VM, VM, VM, ANY, VM, VM, VM, ANY, ANY, ANY, ANY, ANY],
        out_specs=(VM, VM),
        scratch_shapes=[
            pltpu.VMEM((1024, 512), BF16), pltpu.VMEM((3, 1024, 512), BF16),
            pltpu.VMEM((32, 32, 4096), BF16), pltpu.VMEM((3, 512, 2048), BF16),
            pltpu.VMEM((3, 4, 4, 2, 16, 2048), BF16), pltpu.VMEM((512, 4096), BF16),
            pltpu.VMEM((4096, 512), BF16), pltpu.VMEM((512, 4096), BF16),
            pltpu.VMEM((4, 256, 512), BF16), pltpu.VMEM((3, 256, 512), F32),
            pltpu.VMEM((4, 512, 512), BF16), pltpu.VMEM((3, 512, 512), F32),
            pltpu.VMEM((4, 256, 256), F32), pltpu.VMEM((4, 256, 256), BF16),
            pltpu.VMEM((4, 256, 512), F32), pltpu.VMEM((4, 1, 256), F32),
            pltpu.VMEM((4, 32, 1024), BF16), pltpu.VMEM((3, 32, 1024), BF16),
            pltpu.SemaphoreType.DMA((64,)), pltpu.SemaphoreType.DMA((64,)),
            pltpu.SemaphoreType.DMA((7,)),
        ],
        compiler_params=params(3, 60),
    )(*args)


def shards(
    question_ids, answer_ids, owner, slot, passage_score, memory, embedding, live_gain, live_qkv,
    rel_bias, live_out, enc_gain, cross_kv, dec_gain, cross_query, cross_out,
):
    n_psg = lax.axis_size("psg")
    width = live_gain.shape[0]
    plen = memory.shape[1]
    qlen = question_ids.shape[1]
    own_count = owner.shape[1]
    total = own_count * n_psg
    seq = plen + qlen
    cols = live_out.shape[0]

    spread_of = jnp.asarray(spread_table(seq, rel_bias.shape[1]))
    x_mem, token_full, scores, left, right, proj_mem, proj_q, qg, w_val, bias = fetch(
        question_ids, answer_ids, owner.reshape(1, own_count), slot, rel_bias, spread_of, memory,
        embedding, passage_score, live_out,
        jnp.transpose(live_qkv, (1, 0, 2)), cross_kv, cross_query,
        live_gain.reshape(1, width), enc_gain.reshape(1, width), dec_gain.reshape(1, width),
    )
    encoded, decoded = reader(
        proj_mem, proj_q, bias, x_mem.reshape(total, plen, width), token_full, qg, scores,
        left.reshape(3, cols, width // 2), right, live_out, w_val, cross_out,
    )
    return encoded.reshape(1, own_count, seq, width), decoded[None]


def solution(mesh):
    return jax.shard_map(
        shards,
        mesh=mesh,
        in_specs=(
            P("cache", None), P("cache", None), P("cache", "psg", None), P("cache", "psg"),
            P("cache", "psg"), P("cache", None, "psg"), P("cache", "psg"), P(),
            P(None, None, "psg"), P("psg", None), P("psg", None), P(), P(None, None, "psg"), P(),
            P(None, "psg"), P("psg", None),
        ),
        out_specs=(P("cache", "psg", None, None), P("cache", None, "psg")),
        check_vma=False,
    )
```

profile of v0, /device:TPU:1, one launch (start us, length us, event | category | flops | bytes accessed | tf_op | source)
XLA Modules:
  0.0 177.3 jit_solution(4659497066046892491)
XLA Ops:
  0.6 106.7 %shard_map.176 = (bf16[512,4096]{1,0:T(8,128)(2,1)}, bf16[48,4096]{1,0:T(8,128)(2,1)}, f32[4,1,128]{2,1,0:T(1,128)}, bf16[3,4,4,2,16,2048]{5,4,3,2,1,0:T(8,128)(...) custom-call(s32[1,16]{1,0:T(1,128)} %question_ids.1, ...), custom_call_target="tpu_custom_call" | custom-call | tf_op jit(solution)/shard_map/pallas_call | solution.py:611
  107.4 66.1 %shard_map.177 = (bf16[256,4096]{1,0:T(8,128)(2,1)}, bf16[32,1024]{1,0:T(8,128)(2,1)}) custom-call(bf16[3,512,512]{2,1,0:T(8,128)(2,1)} %get-tuple-element.14.proj_mem, bf16[3,16,512]{2,1,0:T(8,128)(2,1)} %get-tuple-element.15.proj_q, f32[8,32,128]{2,1,0:T(8,128)} %get-tuple-element.16.bias, bf16[32,16,4096]{2,1,0:T(8,128)(2,1)} %bitcast.11, ...), custom_call_target="tpu_custom_call" | custom-call | tf_op jit(solution)/shard_map/pallas_call | solution.py:912
  173.5 0.0 copy-start
  173.5 3.2 %copy.21 = bf16[1,8,32,4096]{3,2,1,0:T(8,128)(2,1)} copy(bf16[1,8,32,4096]{3,2,1,0:T(8,128)(2,1)} %bitcast.12) | data formatting | bytes 4194304
  176.6 0.0 copy-done
  176.6 0.6 copy.22
Async XLA Ops:
  173.5 3.2 %copy-start = (bf16[32,1024]{1,0:T(8,128)(2,1)S(1)}, bf16[32,1024]{1,0:T(8,128)(2,1)}, u32[]{:S(2)}) copy-start(bf16[32,1024]{1,0:T(8,128)(2,1)} %get-tuple-element.25) | copy-start | bytes 196612
where the time goes:
time: 177 us
  Pallas kernels  173 us (98%)
  local copies, waits for them, and re-layouts  3.79 us (2%)
    pallas_call x1, Pallas kernels, fetch(): pl.pallas_call(fetch_kernel, out_shape=(jax.ShapeDtypeStruct((512, 4096),...  107 us
    pallas_call x1, Pallas kernels, reader(): pl.pallas_call(reader_kernel, out_shape=(jax.ShapeDtypeStruct((256, 4096)...  66.1 us
    unnamed x4, local copies, waits for them, and re-layouts  3.79 us

commit v1 on v0

--- a/solution.py
+++ b/solution.py
@@ -298,6 +298,11 @@
     mover = Mover(send, recv)
     in_buf = (in_buf0, in_buf1, in_buf2, in_buf3)
 
+    spread = Spread(at, mover, full, 2048)
+    spread.begin(live_out, 0)
+    spread_next = Spread(at, mover, full_next, 2048)
+    spread_next.begin(live_out, 2048)
+
     near = [
         mover.go(every.at[at.c, at.z], every.at[at.c, at.z], at.up(turn(at.z, k)))
         for k in range(1, 4)
@@ -321,10 +326,18 @@
     for copy in near:
         copy.wait_recv()
     lax.fori_loop(1, 32, send_line, 0)
-    spread = Spread(at, mover, full, 2048)
-    spread.begin(live_out, 0)
-    spread_next = Spread(at, mover, full_next, 2048)
-    spread_next.begin(live_out, 2048)
+    split_kv(0, 4)
+    spread.phase_one()
+    spread_next.phase_one()
+    split_kv(4, 6)
+
+    by_bucket = jnp.dot(
+        rel_bias[...], spread_of[...], precision=lax.Precision.HIGHEST, preferred_element_type=F32
+    )
+    for b in range(32):
+        by_key[b] = by_bucket[:, 128 * b : 128 * b + 128]
+    for h in range(8):
+        bias[h] = by_key[:, h, :]
     lax.fori_loop(1, 32, wait_line, 0)
     for q in range(32):
         table[q : q + 1] = (every[q, 0] + every[q, 1]) + (every[q, 2] + every[q, 3])
@@ -363,6 +376,8 @@
 
         def one(d, carry):
             q = lax.rem(at.c + d, 32)
+            if h > 0:
+                passage_copy(h - 1, d).wait_send()
             out_buf[h, 2 * q] = memory[plan[q, 32], :, lanes]
             out_buf[h, 2 * q + 1] = memory[plan[q, 33], :, lanes]
             passage_copy(h, d).start()
@@ -452,8 +467,8 @@
             tok[q // 8, (q // 2) % 4, q % 2] = named[48 * n : 48 * (n + 1)]
     other = 1 - at.core
     pair = mover.go(tok.at[:, :, other], pair_buf, at.sibling())
-    split_kv(0, 3)
-    sent_part(0)
+    spread.phase_one_onward()
+    spread_next.phase_one_onward()
     send_part(1)
 
     pair.wait_recv()
@@ -466,8 +481,13 @@
     lax.fori_loop(0, 4, add_pair, 0)
     wait_part(0)
     rings = [ring_part(0)]
-    sent_part(1)
     send_part(2)
+    wait_part(1)
+    rings.append(ring_part(1))
+    for copy in load_weights:
+        copy.wait()
+    multiply(0, 0)
+    send_part(3)
     lo, hi = pl.ds(0, 512), pl.ds(512, 512)
     tok_a = [
         mover.go(
@@ -485,14 +505,15 @@
         mover.go(score, scores.at[at.z], at.up(turn(at.z, k))) for k in range(1, 4)
     ]
     scores[at.z] = score[...]
-    wait_part(1)
-    rings.append(ring_part(1))
-    for copy in load_weights:
-        copy.wait()
-    multiply(0, 0)
-    sent_part(2)
-    send_part(3)
-    split_kv(3, 6)
+    wait_part(2)
+    rings.append(ring_part(2))
+    rings[0].onward()
+    wait_part(3)
+    rings.append(ring_part(3))
+    spread.phase_one_end()
+    spread_next.phase_one_end()
+    multiply(0, 1)
+    rings[1].onward()
     for copy in tok_a + tok_b:
         copy.wait_recv()
 
@@ -510,11 +531,13 @@
         mover.go(b_buf.at[0, turn(at.x, k)], b2_buf.at[k - 1], at.chip(at.y, turn(at.x, k)))
         for k in range(1, 4)
     ]
-    wait_part(2)
-    rings.append(ring_part(2))
-    rings[0].onward()
-    wait_part(3)
-    rings.append(ring_part(3))
+    spread.phase_two()
+    split_kv(6, 9)
+    rings[0].near()
+    rings[1].near()
+    multiply(1, 0)
+    multiply(-1, 0)
+    rings[2].onward()
     for copy in tok_a2 + tok_b2:
         copy.wait_recv()
     tok_sum[:, lo] = (a2_buf[0] + a2_buf[1]) + (a2_buf[2] + a_buf[0, at.y])
@@ -524,39 +547,13 @@
         mover.go(tok_sum, tokens.at[:, mine], at.up(turn(at.z, k))) for k in range(1, 4)
     ]
     tokens[:, mine] = tok_sum[...]
-    rings[1].onward()
-    spread.phase_one()
-    spread_next.phase_one()
-    multiply(0, 1)
-    split_kv(6, 8)
-    rings[0].near()
-    rings[1].near()
-    multiply(1, 0)
-    spread.phase_one_onward()
-    multiply(-1, 0)
-    split_kv(8, 10)
-    rings[2].onward()
-    spread.phase_one_end()
-    spread.phase_two()
-    spread_next.phase_one_onward()
-    split_kv(10, 13)
-    rings[3].onward()
     rings[0].end()
     rings[1].end()
     multiply(2, 0)
+    rings[3].onward()
+    split_kv(9, 13)
     spread.phase_two_onward()
     split_kv(13, 16)
-    def spread_bias(b, carry):
-        cols = pl.ds(pl.multiple_of(b * 128, 128), 128)
-        by_key[b] = jnp.dot(
-            rel_bias[...], spread_of[:, cols], precision=lax.Precision.HIGHEST,
-            preferred_element_type=F32,
-        )
-        return carry
-
-    lax.fori_loop(0, 32, spread_bias, 0)
-    for h in range(8):
-        bias[h] = by_key[:, h, :]
     keep_values = pltpu.make_async_copy(w_val, w_val_out, local_sem.at[4])
     keep_values.start()
     for copy in near_scores + near_tokens:
@@ -598,7 +595,6 @@
 
     lax.fori_loop(0, 3, close, 0)
     spread.finish()
-    spread_next.phase_one_end()
     for copy in stored:
         copy.wait()
     keep_values.wait()
@@ -691,10 +687,7 @@
     )
 
     low = lax.broadcasted_iota(jnp.int32, (128, 128), 1) < HEAD
-    eye = lax.broadcasted_iota(jnp.int32, (128, 128), 0)
-    eye = eye == lax.broadcasted_iota(jnp.int32, (128, 128), 1)
-    eye = jnp.where(eye, 1.0, 0.0).astype(BF16)
-    owner_lane = lax.broadcasted_iota(jnp.int32, (32, 128), 1) // 32
+    owner_lane = lax.broadcasted_iota(jnp.int32, (32, 256), 1) // 32 % 4
 
     def attend(j):
         def group(g, carry):
@@ -712,23 +705,21 @@
 
             for p in range(4):
                 q, k, v = pair(0, p), pair(1, p), pair(2, p)
-                both = []
-                for e in range(2):
-                    keep = low if e == 0 else jnp.logical_not(low)
-                    full = dot32(k, jnp.where(keep, q, jnp.zeros_like(q)), nt)
-                    sc = full[0:32]
-                    for n in range(1, 4):
-                        sc = jnp.where(owner_lane == n, full[32 * n : 32 * n + 32], sc)
-                    sc = sc * scale + bias[2 * p + e]
-                    ex = jnp.exp(sc - jnp.max(sc, axis=0, keepdims=True))
-                    ex = ex * (1.0 / jnp.sum(ex, axis=0, keepdims=True))
-                    full = jnp.concatenate(
-                        [jnp.where(owner_lane == n, ex, 0.0) for n in range(4)], axis=0
-                    ).astype(BF16)
-                    by_query = dot32(eye, full, nt).astype(BF16)
-                    both.append(jnp.dot(by_query, v, preferred_element_type=F32))
+                none = jnp.zeros_like(q)
+                both = jnp.concatenate([jnp.where(low, q, none), jnp.where(low, none, q)], axis=0)
+                full = dot32(k, both, nt)
+                sc = full[0:32]
+                for n in range(1, 4):
+                    sc = jnp.where(owner_lane == n, full[32 * n : 32 * n + 32], sc)
+                sc = sc * scale + jnp.concatenate([bias[2 * p], bias[2 * p + 1]], axis=1)
+                ex = jnp.exp(sc - jnp.max(sc, axis=0, keepdims=True))
+                ex = ex * (1.0 / jnp.sum(ex, axis=0, keepdims=True))
+                full = jnp.concatenate(
+                    [jnp.where(owner_lane == n, ex, 0.0) for n in range(4)], axis=0
+                ).astype(BF16)
+                out = dot32(full, v, ((0,), (0,)))
                 ctx[pl.ds(pl.multiple_of(first * 32, 128), 128), pl.ds(128 * p, 128)] = jnp.where(
-                    low, both[0], both[1]
+                    low, out[0:128], out[128:256]
                 ).astype(BF16)
             return carry
 

time: 177 us -> 169 us (0.955)
  Pallas kernels: 173 us -> 164 us
    pallas_call x1, Pallas kernels: 107 us -> 100 us  [fetch(): pl.pallas_call(fetch_kernel, out_shape=(jax.ShapeDtypeStruct((512, 4096),...]
    pallas_call x1, Pallas kernels: 66.1 us -> 63.7 us  [reader(): pl.pallas_call(reader_kernel, out_shape=(jax.ShapeDtypeStruct((256, 4096)...]
where the time goes in v1:
time: 169 us; the launch traced here: 168 us
  Pallas kernels  164 us (97%)
  local copies, waits for them, and re-layouts  3.79 us (2%)
    pallas_call x1, Pallas kernels, fetch(): pl.pallas_call(fetch_kernel, out_shape=(jax.ShapeDtypeStruct((512, 4096),...  100 us
    pallas_call x1, Pallas kernels, reader(): pl.pallas_call(reader_kernel, out_shape=(jax.ShapeDtypeStruct((256, 4096)...  63.7 us
    unnamed x4, local copies, waits for them, and re-layouts  3.79 us

profile of v1, /device:TPU:1, one launch (start us, length us, event | category | flops | bytes accessed | tf_op | source)
XLA Modules:
  0.0 168.4 jit_solution(4295113168406261602)
XLA Ops:
  0.6 100.2 %shard_map.176 = (bf16[512,4096]{1,0:T(8,128)(2,1)}, bf16[48,4096]{1,0:T(8,128)(2,1)}, f32[4,1,128]{2,1,0:T(1,128)}, bf16[3,4,4,2,16,2048]{5,4,3,2,1,0:T(8,128)(...) custom-call(s32[1,16]{1,0:T(1,128)} %question_ids.1, ...), custom_call_target="tpu_custom_call" | custom-call | tf_op jit(solution)/shard_map/pallas_call | solution.py:607
  100.9 63.7 %shard_map.177 = (bf16[256,4096]{1,0:T(8,128)(2,1)}, bf16[32,1024]{1,0:T(8,128)(2,1)}) custom-call(bf16[3,512,512]{2,1,0:T(8,128)(2,1)} %get-tuple-element.14.proj_mem, bf16[3,16,512]{2,1,0:T(8,128)(2,1)} %get-tuple-element.15.proj_q, f32[8,32,128]{2,1,0:T(8,128)} %get-tuple-element.16.bias, bf16[32,16,4096]{2,1,0:T(8,128)(2,1)} %bitcast.11, ...), custom_call_target="tpu_custom_call" | custom-call | tf_op jit(solution)/shard_map/pallas_call | solution.py:903
  164.6 0.0 copy-start
  164.6 3.2 %copy.21 = bf16[1,8,32,4096]{3,2,1,0:T(8,128)(2,1)} copy(bf16[1,8,32,4096]{3,2,1,0:T(8,128)(2,1)} %bitcast.12) | data formatting | bytes 4194304
  167.7 0.0 copy-done
  167.7 0.6 copy.22
Async XLA Ops:
  164.6 3.2 %copy-start = (bf16[32,1024]{1,0:T(8,128)(2,1)S(1)}, bf16[32,1024]{1,0:T(8,128)(2,1)}, u32[]{:S(2)}) copy-start(bf16[32,1024]{1,0:T(8,128)(2,1)} %get-tuple-element.25) | copy-start | bytes 196612

commit v2 on v1

--- a/solution.py
+++ b/solution.py
@@ -651,8 +651,8 @@
 def reader_kernel(
     proj_mem, proj_q, bias, x_mem, tokens, qg, scores, left_in, right_in, live_out, w_val_in,
     cross_out_in,
-    encoded, decoded,
-    ctx, others, x_seq, left, right, own_out, w_val, w_out, ql, ql_part, lv, lv_part, s, w, values,
+    encoded_out, decoded,
+    encoded, ctx, others, x_seq, left, right, own_out, w_val, w_out, ql, ql_part, lv, lv_part, s, w, values,
     inv, parts, part_buf, send, recv, local_sem,
 ):
     at = Place()
@@ -672,10 +672,6 @@
     greet_all(at)
     scale = HEAD ** (-0.5)
     nt = ((1,), (1,))
-    loads[0].wait()
-    loads[1].wait()
-    spread.phase_two()
-
     def chunk(j):
         return pl.ds(pl.multiple_of(j * 256, 256), 256)
 
@@ -729,6 +725,10 @@
         attend(turn(at.z, u))
         ring.begin_right(u)
         ring.begin_left(u)
+        if u == 2:
+            loads[0].wait()
+            loads[1].wait()
+            spread.phase_two()
 
     loads[2].wait()
 
@@ -737,7 +737,6 @@
         return carry
 
     lax.fori_loop(0, 32, fill, 0)
-    ring.pass_right(2)
 
     def rows_of(j):
         return x_seq[pl.ds(j * 8, 8)].reshape(256, 4096)
@@ -747,8 +746,6 @@
         return carry
 
     lax.fori_loop(0, 4, score_inputs, 0)
-    ring.pass_left(3)
-    spread.phase_two_onward()
     loads[4].wait()
     of_question = jnp.dot(tokens[pl.ds(0, 16)], w_val[...], preferred_element_type=F32)
 
@@ -763,7 +760,6 @@
         return carry
 
     lax.fori_loop(0, 4, value_inputs, 0)
-    ring.pass_right(1)
     loads[3].wait()
     ql[0] = dot32(qg[...], own_out[...], nt).astype(BF16)
     lv[0] = jnp.dot(own_out[...], w_val[...], preferred_element_type=F32).astype(BF16)
@@ -777,6 +773,7 @@
         return carry
 
     lax.fori_loop(0, 4, absorb_own, 0)
+    spread.phase_two_onward()
     loads[5].wait()
     half, rest = pl.ds(0, 2048), pl.ds(2048, 2048)
 
@@ -786,7 +783,9 @@
         return carry
 
     lax.fori_loop(0, 3, fold_left, 0)
-    ring.pass_left(0)
+    ring.pass_right(2)
+    ring.pass_left(3)
+    ring.pass_right(1)
     spread.finish()
 
     def fold_right(k, carry):
@@ -798,6 +797,8 @@
         return carry
 
     lax.fori_loop(0, 3, fold_right, 0)
+
+    ring.pass_left(0)
 
     ring.far[2].wait_recv()
     mine = chunk(at.z)
@@ -823,6 +824,8 @@
         encoded[:, cols] = own_rows
         own_rows = own_rows.astype(F32)
         squares = squares + jnp.sum(own_rows * own_rows, axis=1, keepdims=True)
+    keep = pltpu.make_async_copy(encoded, encoded_out, local_sem.at[7])
+    keep.start()
     norm = lax.rsqrt(squares * (1.0 / 4096) + EPSILON)
     inv[at.z] = jnp.transpose(jnp.broadcast_to(norm, (256, 128)))[0:1]
     near = [mover.go(inv.at[at.z], inv.at[at.z], at.up(turn(at.z, k))) for k in range(1, 4)]
@@ -896,6 +899,7 @@
     for k in range(3):
         total = total + part_buf[k].astype(F32)
     decoded[...] = total.astype(BF16)
+    keep.wait()
     mover.finish_sends()
 
 
@@ -907,8 +911,9 @@
             jax.ShapeDtypeStruct((32, 1024), BF16),
         ),
         in_specs=[VM, VM, VM, ANY, VM, VM, VM, ANY, ANY, ANY, ANY, ANY],
-        out_specs=(VM, VM),
+        out_specs=(ANY, VM),
         scratch_shapes=[
+            pltpu.VMEM((256, 4096), BF16),
             pltpu.VMEM((1024, 512), BF16), pltpu.VMEM((3, 1024, 512), BF16),
             pltpu.VMEM((32, 32, 4096), BF16), pltpu.VMEM((3, 512, 2048), BF16),
             pltpu.VMEM((3, 4, 4, 2, 16, 2048), BF16), pltpu.VMEM((512, 4096), BF16),
@@ -919,7 +924,7 @@
             pltpu.VMEM((4, 256, 512), F32), pltpu.VMEM((4, 1, 256), F32),
             pltpu.VMEM((4, 32, 1024), BF16), pltpu.VMEM((3, 32, 1024), BF16),
             pltpu.SemaphoreType.DMA((64,)), pltpu.SemaphoreType.DMA((64,)),
-            pltpu.SemaphoreType.DMA((7,)),
+            pltpu.SemaphoreType.DMA((8,)),
         ],
         compiler_params=params(3, 60),
     )(*args)

time: 169 us -> 162 us (0.959)
  Pallas kernels: 164 us -> 158 us
    pallas_call x1, Pallas kernels: 63.7 us -> 57.3 us  [reader(): pl.pallas_call(reader_kernel, out_shape=(jax.ShapeDtypeStruct((256, 4096)...]
where the time goes in v2:
time: 162 us
  Pallas kernels  158 us (98%)
  local copies, waits for them, and re-layouts  3.79 us (2%)
    pallas_call x1, Pallas kernels, fetch(): pl.pallas_call(fetch_kernel, out_shape=(jax.ShapeDtypeStruct((512, 4096),...  100 us
    pallas_call x1, Pallas kernels, reader(): pl.pallas_call(reader_kernel, out_shape=(jax.ShapeDtypeStruct((256, 4096)...  57.3 us
    unnamed x4, local copies, waits for them, and re-layouts  3.79 us

profile of v2, /device:TPU:1, one launch (start us, length us, event | category | flops | bytes accessed | tf_op | source)
XLA Modules:
  0.0 162.0 jit_solution(11578536863725284585)
XLA Ops:
  0.6 100.2 %shard_map.176 = (bf16[512,4096]{1,0:T(8,128)(2,1)}, bf16[48,4096]{1,0:T(8,128)(2,1)}, f32[4,1,128]{2,1,0:T(1,128)}, bf16[3,4,4,2,16,2048]{5,4,3,2,1,0:T(8,128)(...) custom-call(s32[1,16]{1,0:T(1,128)} %question_ids.1, ...), custom_call_target="tpu_custom_call" | custom-call | tf_op jit(solution)/shard_map/pallas_call | solution.py:607
  100.9 57.3 %shard_map.177 = (bf16[256,4096]{1,0:T(8,128)(2,1)}, bf16[32,1024]{1,0:T(8,128)(2,1)}) custom-call(bf16[3,512,512]{2,1,0:T(8,128)(2,1)} %get-tuple-element.14.proj_mem, bf16[3,16,512]{2,1,0:T(8,128)(2,1)} %get-tuple-element.15.proj_q, f32[8,32,128]{2,1,0:T(8,128)} %get-tuple-element.16.bias, bf16[32,16,4096]{2,1,0:T(8,128)(2,1)} %bitcast.11, ...), custom_call_target="tpu_custom_call" | custom-call | tf_op jit(solution)/shard_map/pallas_call | solution.py:907
  158.2 0.0 copy-start
  158.2 3.2 %copy.21 = bf16[1,8,32,4096]{3,2,1,0:T(8,128)(2,1)} copy(bf16[1,8,32,4096]{3,2,1,0:T(8,128)(2,1)} %bitcast.12) | data formatting | bytes 4194304
  161.3 0.0 copy-done
  161.3 0.6 copy.22
Async XLA Ops:
  158.2 3.2 %copy-start = (bf16[32,1024]{1,0:T(8,128)(2,1)S(1)}, bf16[32,1024]{1,0:T(8,128)(2,1)}, u32[]{:S(2)}) copy-start(bf16[32,1024]{1,0:T(8,128)(2,1)} %get-tuple-element.25) | copy-start | bytes 196612

commit v3 on v2

--- a/solution.py
+++ b/solution.py
@@ -245,9 +245,9 @@
     question_ids, answer_ids, owner, slot, rel_bias, spread_of, memory, embedding, own_score,
     live_out, w_qkv, cross_kv, cross_query,
     live_gain, enc_gain, dec_gain,
-    x_out, tokens, scores, full, full_next, proj_mem, proj_q, qg, w_val_out, bias,
+    x_out, tokens, scores, full, full_next, proj_mem, proj_q, qg_out, w_val_out, bias,
     line_buf, score, by_key, every, table, turned, plan, tok, table_w, out_buf, in_buf0, in_buf1, in_buf2, in_buf3, own, pair_buf, a_buf, b_buf, a2_buf, b2_buf, tok_sum,
-    x_full, weights, acc, squares, scaled, w_query, kv_buf, w_key, w_val,
+    qg, x_full, weights, acc, squares, scaled, w_query, kv_buf, w_key, w_val,
     send, recv, a2a_send, a2a_recv, line_send, line_recv, local_sem, kv_sem, out_sem,
 ):
     at = Place()
@@ -484,9 +484,6 @@
     send_part(2)
     wait_part(1)
     rings.append(ring_part(1))
-    for copy in load_weights:
-        copy.wait()
-    multiply(0, 0)
     send_part(3)
     lo, hi = pl.ds(0, 512), pl.ds(512, 512)
     tok_a = [
@@ -510,10 +507,13 @@
     rings[0].onward()
     wait_part(3)
     rings.append(ring_part(3))
+    rings[1].onward()
     spread.phase_one_end()
     spread_next.phase_one_end()
+    for copy in load_weights:
+        copy.wait()
+    multiply(0, 0)
     multiply(0, 1)
-    rings[1].onward()
     for copy in tok_a + tok_b:
         copy.wait_recv()
 
@@ -580,6 +580,8 @@
         return carry
 
     lax.fori_loop(0, 4, fold, 0)
+    keep_folded = pltpu.make_async_copy(qg, qg_out, local_sem.at[7])
+    keep_folded.start()
     rings[2].near()
     rings[3].near()
     multiply(1, 1)
@@ -598,6 +600,7 @@
     for copy in stored:
         copy.wait()
     keep_values.wait()
+    keep_folded.wait()
     mover.finish_sends()
 
     sent_part(3)
@@ -619,7 +622,7 @@
             jax.ShapeDtypeStruct((8, 32, 128), F32),
         ),
         in_specs=[VM] * 7 + [ANY, VM, ANY, ANY, ANY, ANY, VM, VM, VM],
-        out_specs=(ANY, VM, VM, ANY, ANY, VM, VM, VM, ANY, VM),
+        out_specs=(ANY, VM, VM, ANY, ANY, VM, VM, ANY, ANY, VM),
         scratch_shapes=[
             pltpu.VMEM((8, 128), jnp.int32), pltpu.VMEM((1, 128), F32),
             pltpu.VMEM((32, 8, 128), F32),
@@ -633,6 +636,7 @@
             pltpu.VMEM((3, 4, 48, 512), BF16), pltpu.VMEM((3, 4, 48, 512), BF16),
             pltpu.VMEM((3, 48, 512), BF16), pltpu.VMEM((3, 48, 512), BF16),
             pltpu.VMEM((48, 1024), BF16),
+            pltpu.VMEM((256, 4096), BF16),
             pltpu.VMEM((512, 4096), BF16), pltpu.VMEM((3, 4096, 512), BF16),
             pltpu.VMEM((3, 512, 512), F32), pltpu.VMEM((512, 1), F32),
             pltpu.VMEM((512, 512), BF16), pltpu.VMEM((4096, 512), BF16),
@@ -641,7 +645,7 @@
             pltpu.SemaphoreType.DMA((112,)), pltpu.SemaphoreType.DMA((112,)),
             pltpu.SemaphoreType.DMA((4, 32)), pltpu.SemaphoreType.DMA((4, 32)),
             pltpu.SemaphoreType.DMA((32,)), pltpu.SemaphoreType.DMA((32,)),
-            pltpu.SemaphoreType.DMA((7,)), pltpu.SemaphoreType.DMA((4,)),
+            pltpu.SemaphoreType.DMA((8,)), pltpu.SemaphoreType.DMA((4,)),
             pltpu.SemaphoreType.DMA((8,)),
         ],
         compiler_params=params(2, 60),
@@ -649,10 +653,10 @@
 
 
 def reader_kernel(
-    proj_mem, proj_q, bias, x_mem, tokens, qg, scores, left_in, right_in, live_out, w_val_in,
+    proj_mem, proj_q, bias, x_mem, tokens, qg_in, scores, left_in, right_in, live_out, w_val_in,
     cross_out_in,
     encoded_out, decoded,
-    encoded, ctx, others, x_seq, left, right, own_out, w_val, w_out, ql, ql_part, lv, lv_part, s, w, values,
+    qg, encoded, ctx, others, x_seq, left, right, own_out, w_val, w_out, ql, ql_part, lv, lv_part, s, w, values,
     inv, parts, part_buf, send, recv, local_sem,
 ):
     at = Place()
@@ -664,7 +668,7 @@
             (spread.line(right_in, "x"), spread.line(right, "x")),
             (spread.line(right_in, "y"), spread.line(right, "y")),
             (x_mem, x_seq.at[:, pl.ds(0, 16)]), (live_out, own_out), (w_val_in, w_val),
-            (left_in, left), (cross_out_in, w_out),
+            (left_in, left), (cross_out_in, w_out), (qg_in, qg),
         ])
     ]
     for copy in loads:
@@ -731,6 +735,7 @@
             spread.phase_two()
 
     loads[2].wait()
+    loads[7].wait()
 
     def fill(p, carry):
         x_seq[p, pl.ds(16, 16)] = tokens[pl.ds(0, 16)]
@@ -760,6 +765,7 @@
         return carry
 
     lax.fori_loop(0, 4, value_inputs, 0)
+    spread.phase_two_onward()
     loads[3].wait()
     ql[0] = dot32(qg[...], own_out[...], nt).astype(BF16)
     lv[0] = jnp.dot(own_out[...], w_val[...], preferred_element_type=F32).astype(BF16)
@@ -773,7 +779,6 @@
         return carry
 
     lax.fori_loop(0, 4, absorb_own, 0)
-    spread.phase_two_onward()
     loads[5].wait()
     half, rest = pl.ds(0, 2048), pl.ds(2048, 2048)
 
@@ -824,7 +829,7 @@
         encoded[:, cols] = own_rows
         own_rows = own_rows.astype(F32)
         squares = squares + jnp.sum(own_rows * own_rows, axis=1, keepdims=True)
-    keep = pltpu.make_async_copy(encoded, encoded_out, local_sem.at[7])
+    keep = pltpu.make_async_copy(encoded, encoded_out, local_sem.at[8])
     keep.start()
     norm = lax.rsqrt(squares * (1.0 / 4096) + EPSILON)
     inv[at.z] = jnp.transpose(jnp.broadcast_to(norm, (256, 128)))[0:1]
@@ -910,10 +915,10 @@
             jax.ShapeDtypeStruct((256, 4096), BF16),
             jax.ShapeDtypeStruct((32, 1024), BF16),
         ),
-        in_specs=[VM, VM, VM, ANY, VM, VM, VM, ANY, ANY, ANY, ANY, ANY],
+        in_specs=[VM, VM, VM, ANY, VM, ANY, VM, ANY, ANY, ANY, ANY, ANY],
         out_specs=(ANY, VM),
         scratch_shapes=[
-            pltpu.VMEM((256, 4096), BF16),
+            pltpu.VMEM((256, 4096), BF16), pltpu.VMEM((256, 4096), BF16),
             pltpu.VMEM((1024, 512), BF16), pltpu.VMEM((3, 1024, 512), BF16),
             pltpu.VMEM((32, 32, 4096), BF16), pltpu.VMEM((3, 512, 2048), BF16),
             pltpu.VMEM((3, 4, 4, 2, 16, 2048), BF16), pltpu.VMEM((512, 4096), BF16),
@@ -924,7 +929,7 @@
             pltpu.VMEM((4, 256, 512), F32), pltpu.VMEM((4, 1, 256), F32),
             pltpu.VMEM((4, 32, 1024), BF16), pltpu.VMEM((3, 32, 1024), BF16),
             pltpu.SemaphoreType.DMA((64,)), pltpu.SemaphoreType.DMA((64,)),
-            pltpu.SemaphoreType.DMA((8,)),
+            pltpu.SemaphoreType.DMA((9,)),
         ],
         compiler_params=params(3, 60),
     )(*args)

time: 162 us -> 159 us (0.981)
  Pallas kernels: 158 us -> 154 us
    pallas_call x1, Pallas kernels: 57.3 us -> 54.5 us  [reader(): pl.pallas_call(reader_kernel, out_shape=(jax.ShapeDtypeStruct((256, 4096)...]
where the time goes in v3:
time: 159 us; the launch traced here: 158 us
  Pallas kernels  154 us (97%)
  local copies, waits for them, and re-layouts  3.79 us (2%)
    pallas_call x1, Pallas kernels, fetch(): pl.pallas_call(fetch_kernel, out_shape=(jax.ShapeDtypeStruct((512, 4096),...  99.4 us
    pallas_call x1, Pallas kernels, reader(): pl.pallas_call(reader_kernel, out_shape=(jax.ShapeDtypeStruct((256, 4096)...  54.5 us
    unnamed x4, local copies, waits for them, and re-layouts  3.79 us

profile of v3, /device:TPU:1, one launch (start us, length us, event | category | flops | bytes accessed | tf_op | source)
XLA Modules:
  0.0 158.3 jit_solution(11166605079770283707)
XLA Ops:
  0.6 99.4 %shard_map.176 = (bf16[512,4096]{1,0:T(8,128)(2,1)}, bf16[48,4096]{1,0:T(8,128)(2,1)}, f32[4,1,128]{2,1,0:T(1,128)}, bf16[3,4,4,2,16,2048]{5,4,3,2,1,0:T(8,128)(...) custom-call(s32[1,16]{1,0:T(1,128)} %question_ids.1, ...), custom_call_target="tpu_custom_call" | custom-call | tf_op jit(solution)/shard_map/pallas_call | solution.py:610
  100.0 54.5 %shard_map.177 = (bf16[256,4096]{1,0:T(8,128)(2,1)}, bf16[32,1024]{1,0:T(8,128)(2,1)}) custom-call(bf16[3,512,512]{2,1,0:T(8,128)(2,1)} %get-tuple-element.14.proj_mem, bf16[3,16,512]{2,1,0:T(8,128)(2,1)} %get-tuple-element.15.proj_q, f32[8,32,128]{2,1,0:T(8,128)} %get-tuple-element.16.bias, bf16[32,16,4096]{2,1,0:T(8,128)(2,1)} %bitcast.11, ...), custom_call_target="tpu_custom_call" | custom-call | tf_op jit(solution)/shard_map/pallas_call | solution.py:912
  154.5 0.0 copy-start
  154.5 3.2 %copy.21 = bf16[1,8,32,4096]{3,2,1,0:T(8,128)(2,1)} copy(bf16[1,8,32,4096]{3,2,1,0:T(8,128)(2,1)} %bitcast.12) | data formatting | bytes 4194304
  157.7 0.0 copy-done
  157.7 0.6 copy.22
Async XLA Ops:
  154.5 3.2 %copy-start = (bf16[32,1024]{1,0:T(8,128)(2,1)S(1)}, bf16[32,1024]{1,0:T(8,128)(2,1)}, u32[]{:S(2)}) copy-start(bf16[32,1024]{1,0:T(8,128)(2,1)} %get-tuple-element.25) | copy-start | bytes 196612

commit v4 on v3

--- a/solution.py
+++ b/solution.py
@@ -535,9 +535,9 @@
     split_kv(6, 9)
     rings[0].near()
     rings[1].near()
+    rings[2].onward()
     multiply(1, 0)
     multiply(-1, 0)
-    rings[2].onward()
     for copy in tok_a2 + tok_b2:
         copy.wait_recv()
     tok_sum[:, lo] = (a2_buf[0] + a2_buf[1]) + (a2_buf[2] + a_buf[0, at.y])
@@ -547,10 +547,10 @@
         mover.go(tok_sum, tokens.at[:, mine], at.up(turn(at.z, k))) for k in range(1, 4)
     ]
     tokens[:, mine] = tok_sum[...]
+    rings[3].onward()
     rings[0].end()
     rings[1].end()
     multiply(2, 0)
-    rings[3].onward()
     split_kv(9, 13)
     spread.phase_two_onward()
     split_kv(13, 16)

time: 159 us -> 157 us (0.987)
  Pallas kernels: 154 us -> 152 us
    pallas_call x1, Pallas kernels: 54.5 us -> 52.8 us  [reader(): pl.pallas_call(reader_kernel, out_shape=(jax.ShapeDtypeStruct((256, 4096)...]
where the time goes in v4:
time: 157 us
  Pallas kernels  152 us (97%)
  local copies, waits for them, and re-layouts  3.79 us (2%)
    pallas_call x1, Pallas kernels, fetch(): pl.pallas_call(fetch_kernel, out_shape=(jax.ShapeDtypeStruct((512, 4096),...  99.4 us
    pallas_call x1, Pallas kernels, reader(): pl.pallas_call(reader_kernel, out_shape=(jax.ShapeDtypeStruct((256, 4096)...  52.8 us
    unnamed x4, local copies, waits for them, and re-layouts  3.79 us

profile of v4, /device:TPU:1, one launch (start us, length us, event | category | flops | bytes accessed | tf_op | source)
XLA Modules:
  0.0 156.6 jit_solution(7916971016832865311)
XLA Ops:
  0.6 99.4 %shard_map.176 = (bf16[512,4096]{1,0:T(8,128)(2,1)}, bf16[48,4096]{1,0:T(8,128)(2,1)}, f32[4,1,128]{2,1,0:T(1,128)}, bf16[3,4,4,2,16,2048]{5,4,3,2,1,0:T(8,128)(...) custom-call(s32[1,16]{1,0:T(1,128)} %question_ids.1, ...), custom_call_target="tpu_custom_call" | custom-call | tf_op jit(solution)/shard_map/pallas_call | solution.py:610
  100.0 52.8 %shard_map.177 = (bf16[256,4096]{1,0:T(8,128)(2,1)}, bf16[32,1024]{1,0:T(8,128)(2,1)}) custom-call(bf16[3,512,512]{2,1,0:T(8,128)(2,1)} %get-tuple-element.14.proj_mem, bf16[3,16,512]{2,1,0:T(8,128)(2,1)} %get-tuple-element.15.proj_q, f32[8,32,128]{2,1,0:T(8,128)} %get-tuple-element.16.bias, bf16[32,16,4096]{2,1,0:T(8,128)(2,1)} %bitcast.11, ...), custom_call_target="tpu_custom_call" | custom-call | tf_op jit(solution)/shard_map/pallas_call | solution.py:912
  152.8 0.0 copy-start
  152.8 3.2 %copy.21 = bf16[1,8,32,4096]{3,2,1,0:T(8,128)(2,1)} copy(bf16[1,8,32,4096]{3,2,1,0:T(8,128)(2,1)} %bitcast.12) | data formatting | bytes 4194304
  156.0 0.0 copy-done
  156.0 0.6 copy.22
Async XLA Ops:
  152.8 3.2 %copy-start = (bf16[32,1024]{1,0:T(8,128)(2,1)S(1)}, bf16[32,1024]{1,0:T(8,128)(2,1)}, u32[]{:S(2)}) copy-start(bf16[32,1024]{1,0:T(8,128)(2,1)} %get-tuple-element.25) | copy-start | bytes 196612
